TPU v7x, 32 devices: a whole 2x2x4 slice. The times are simulated.
32 devices in a mesh: grp: 2 (over x), cell: 16 (over z, y, core).
Axes of the slice: x: 2, y: 2, z: 4, core: 2. Of those that a mesh axis runs over, the one named last changes fastest.
Arguments:
- fields: bfloat16 [8192, 3, 8192], P(('grp', 'cell')), parts along dimension 0, may hold values from -6 to 6
- horiz: float32 [16384], P(('grp', 'cell')), parts along dimension 0, may hold values from 0.2 to 1
- vertical: float32 [16384], P(('grp', 'cell')), parts along dimension 0, may hold values from 1.5 to 6
- tilt_angle: float32 [16384], P(('grp', 'cell')), parts along dimension 0, may hold values from 0.2 to 1.4
- azimuth: float32 [16384], P(('grp', 'cell')), parts along dimension 0, may hold values from -3.140625 to 3.140625
- electrode_quads: int32 [4096, 4], P('grp'), parts along dimension 0, may hold values from 0 to 4095, as said below
Outputs:
- jacobian: bfloat16 [4096, 4, 8192], P('grp', None, 'cell'), parts along dimension 0
- coverage: float32 [16384], P(('grp', 'cell')), parts along dimension 0
There are 2 independent parts, one for each index of `grp`. A program takes and returns all parts, laid end to end along the dimension named above; each array names one. Nothing has to cross between parts.
Inputs may be any that keep to these rules, and one draw needn't show every extreme that they name: `electrode_quads`: each row names four different electrodes.
All inputs are finite; a program needn't handle non-finite values.
Results may differ from a plain program's by a relative error of at most 0.001.
Values may be sent and summed in bfloat16 or wider, within the bound.
A program may use at most 192 MiB of HBM per device.

v0:
```python
import jax
import jax.numpy as jnp
from jax import lax
from jax.sharding import PartitionSpec as P


def sensitivity(grads, horiz, vertical, tilt_angle, azimuth, rows):

    def pick(column):
        return jnp.take(grads, rows[:, column], axis=0).astype(jnp.float32)

    source = pick(0) - pick(1)
    receiver = pick(2) - pick(3)
    sin_t = jnp.sin(tilt_angle)
    cos_t = jnp.cos(tilt_angle)
    sin_p = jnp.sin(azimuth)
    cos_p = jnp.cos(azimuth)
    axis_dir = jnp.stack([sin_t * cos_p, sin_t * sin_p, cos_t])
    tilt_dir = jnp.stack([cos_t * cos_p, cos_t * sin_p, -sin_t])
    turn_dir = jnp.stack([-sin_t * sin_p, sin_t * cos_p, jnp.zeros_like(sin_t)])

    def along(field, direction):
        return jnp.sum(field * direction[None], axis=1)

    s_axis = along(source, axis_dir)
    r_axis = along(receiver, axis_dir)
    s_tilt = along(source, tilt_dir)
    r_tilt = along(receiver, tilt_dir)
    s_turn = along(source, turn_dir)
    r_turn = along(receiver, turn_dir)
    inner = jnp.sum(source * receiver, axis=1)
    contrast = vertical - horiz
    return jnp.stack(
        [
            -horiz * (inner - s_axis * r_axis),
            -vertical * s_axis * r_axis,
            -contrast * (s_tilt * r_axis + s_axis * r_tilt),
            -contrast * (s_turn * r_axis + s_axis * r_turn),
        ],
        axis=1,
    )


def local(fields, horiz, vertical, tilt_angle, azimuth, electrode_quads):
    shards = lax.axis_size("cell")
    cell_dev = horiz.shape[0]
    local_fields = lax.all_to_all(fields, "cell", split_axis=2, concat_axis=0, tiled=True)
    values = sensitivity(local_fields, horiz, vertical, tilt_angle, azimuth, electrode_quads)
    partial_sq = jnp.sum(values * values, axis=(1, 2))
    total_sq = lax.psum(partial_sq, "cell")
    meansq = total_sq / (4.0 * cell_dev * shards)
    normed = values * lax.rsqrt(meansq + 1e-06)[:, None, None]
    return (normed.astype(jnp.bfloat16), jnp.sum(normed * normed, axis=(0, 1)))


def solution(mesh):
    placed = (
        P(("grp", "cell"), None, None),
        P(("grp", "cell")),
        P(("grp", "cell")),
        P(("grp", "cell")),
        P(("grp", "cell")),
        P("grp", None),
    )
    return jax.shard_map(
        local,
        mesh=mesh,
        in_specs=placed,
        out_specs=(P("grp", None, "cell"), P(("grp", "cell"))),
        check_vma=False,
    )
```

profile of v0, /device:TPU:0, one launch (start us, length us, event | category | flops | bytes accessed | tf_op | source)
XLA Modules:
  0.0 745.1 jit_solution(583494292606352755)
XLA Ops:
  0.6 25.0 %copy.16 = bf16[256,3,8192]{0,1,2:T(4,128)(2,1)} copy(bf16[256,3,8192]{2,0,1:T(8,128)(2,1)} %param.8) | data formatting | bytes 25165824 | tf_op args[0]
  25.6 0.0 copy-start.5
  25.6 0.0 copy-start.6
  25.6 0.0 copy-start.3
  25.6 0.0 copy-start.4
  25.6 0.0 copy-start.2
  25.6 7.6 %all-to-all-start = ((bf16[256,3,8192]{0,1,2:T(4,128)(2,1)}), bf16[256,3,8192]{0,1,2:T(4,128)(2,1)}, u32[]{:S(2)}, u32[]{:S(2)}) async-start(bf16[256,3,8192]{0,1,2:T(4,128)(2,1)} %copy.16), calls=%async_computation | async-start | bytes 33554432 | tf_op jit(solution)/shard_map/all_to_all | solution.py:47
  33.2 0.1 pad.6.clone
  33.3 0.0 copy-done.5
  33.3 0.0 copy-done.6
  33.4 0.0 copy-done.3
  33.4 0.0 copy-done.4
  33.4 0.0 copy-done.2
  33.5 0.1 pad_maximum_fusion.1
  33.6 296.4 %all-to-all-done = bf16[256,3,8192]{0,1,2:T(4,128)(2,1)} async-done(((bf16[256,3,8192]{0,1,2:T(4,128)(2,1)}), bf16[256,3,8192]{0,1,2:T(4,128)(2,1)}, u32[]{:S(2)}, u32[]{:S(2)}) %all-to-all-start) | async-done | bytes 12582944 | tf_op jit(solution)/shard_map/all_to_all | solution.py:47
  330.0 13.2 %copy.17 = bf16[256,3,8192]{0,2,1:T(8,128)(2,1)} copy(bf16[256,3,8192]{0,1,2:T(4,128)(2,1)} %all-to-all-done) | data formatting | bytes 25165824 | tf_op jit(solution)/shard_map/all_to_all | solution.py:47
  343.1 16.6 %copy.18 = bf16[16,256,3,512]{3,1,0,2:T(8,128)(2,1)} copy(bf16[16,256,3,512]{1,3,0,2:T(8,128)(2,1)} %bitcast.54) | data formatting | bytes 25165824 | tf_op jit(solution)/shard_map/all_to_all | solution.py:47
  359.7 18.9 %copy.19 = bf16[4096,3,512]{2,1,0:T(4,128)(2,1)} copy(bf16[4096,3,512]{2,0,1:T(8,128)(2,1)} %bitcast.55) | data formatting | bytes 25165824 | tf_op jit(solution)/shard_map/all_to_all | solution.py:47
  378.6 26.7 %gather_fusion = bf16[2048,3,512]{2,1,0:T(4,128)(2,1)} fusion(bf16[4096,3,512]{2,1,0:T(4,128)(2,1)} %copy.19, s32[2048]{0:T(1024)S(1)} %fusion.6), kind=kCustom, calls=%fused_computation.clone | custom fusion | bytes 12591104 | tf_op jit(solution)/shard_map/jit(_take)/gather | solution.py:10
  405.2 26.9 %gather_fusion.1 = bf16[2048,3,512]{2,1,0:T(4,128)(2,1)} fusion(bf16[4096,3,512]{2,1,0:T(4,128)(2,1)} %copy.19, s32[2048]{0:T(1024)S(1)} %fusion.7), kind=kCustom, calls=%fused_computation.1.clone | custom fusion | bytes 12591104 | tf_op jit(solution)/shard_map/jit(_take)/gather | solution.py:10
  432.1 27.0 %gather_fusion.2 = bf16[2048,3,512]{2,1,0:T(4,128)(2,1)} fusion(bf16[4096,3,512]{2,1,0:T(4,128)(2,1)} %copy.19, s32[2048]{0:T(1024)S(1)} %fusion.8), kind=kCustom, calls=%fused_computation.2.clone | custom fusion | bytes 12591104 | tf_op jit(solution)/shard_map/jit(_take)/gather | solution.py:10
  459.1 26.8 %gather_fusion.3 = bf16[2048,3,512]{2,1,0:T(4,128)(2,1)} fusion(bf16[4096,3,512]{2,1,0:T(4,128)(2,1)} %copy.19, s32[2048]{0:T(1024)S(1)} %fusion.9), kind=kCustom, calls=%fused_computation.3.clone | custom fusion | bytes 12591104 | tf_op jit(solution)/shard_map/jit(_take)/gather | solution.py:10
  485.9 103.7 %multiply_reduce_fusion.8 = (f32[2048,512]{1,0:T(8,128)}, f32[2048,512]{1,0:T(8,128)}, f32[2048,512]{1,0:T(8,128)}, f32[2048,512]{1,0:T(8,128)}, f32[2048,512]{1...) fusion(bf16[2048,3,512]{2,1,0:T(4,128)(2,1)} %gather_fusion, pred[2048]{0:T(1024)(128)(4,1)S(1)} %get-tuple-element.48, ...), kind=kLoop, calls=%fused_computation.13 | loop fusion | flops 68157440 | bytes 54552576 | tf_op jit(solution)/shard_map/reduce_sum | solution.py:31
  589.6 14.0 %fusion.5 = (f32[2048,1,512]{2,0,1:T(8,128)S(1)}, f32[2048,1,512]{2,0,1:T(8,128)S(1)}, f32[2048,1,512]{2,0,1:T(8,128)}, f32[2048,1,512]{2,0,1:T(8,128)}) fusion(f32[2048,512]{1,0:T(8,128)} %get-tuple-element.14, f32[2048,512]{1,0:T(8,128)} %get-tuple-element.15, f32[2048,512]{1,0:T(8,128)} %get-tuple-element.9, f32[512]{0:T(512)S(1)} %get-tuple-element.34, ...), kind=kLoop, calls=%fused_computation.32 | loop fusion | flops 13631488 | bytes 46143488 | tf_op jit(solution)/shard_map/mul | solution.py:35
  603.6 0.0 copy-start
  603.6 0.0 copy-start.1
  603.6 2.0 copy-done
  605.5 1.2 copy-done.1
  606.8 4.6 multiply_reduce_fusion.1
  611.4 98.9 %psum.7 = f32[2048]{0:T(1024)S(1)} all-reduce(f32[2048]{0:T(1024)S(1)} %multiply_reduce_fusion.1), channel_id=1, replica_groups=mesh['grp'=2,'cell'=16] {'cell'}, use_global_device_ids=true, to_apply=%region_8.10 | all-reduce | flops 2048 | bytes 16384 | tf_op jit(solution)/shard_map/psum | solution.py:50
  710.3 7.5 %multiply_reduce_fusion = (f32[512]{0:T(512)}, bf16[2048,4,512]{2,0,1:T(8,128)(2,1)S(1)}) fusion(f32[2048]{0:T(1024)S(1)} %add_rsqrt_fusion, f32[2048,1,512]{2,0,1:T(8,128)} %get-tuple-element.22, f32[2048,1,512]{2,0,1:T(8,128)} %get-tuple-element.23, f32[2048,1,512]{2,0,1:T(8,128)} %copy-done.1, f32[2048,1,512]{2,0,1:T(8,128)} %copy-done), kind=kLoop, calls=%fused_computation.5 | loop fusion | flops 29359616 | bytes 25176064 | tf_op jit(solution)/shard_map/reduce_sum | solution.py:53
  717.8 27.3 %copy.23 = bf16[2048,4,512]{2,1,0:T(4,128)(2,1)} copy(bf16[2048,4,512]{2,0,1:T(8,128)(2,1)S(1)} %get-tuple-element.17) | data formatting | bytes 16777216
  (12 shorter events, 0.2 us)
Async XLA Ops:
  25.6 7.7 %copy-start.5 = (f32[512]{0:T(512)S(1)}, f32[512]{0:T(512)}, u32[]{:S(2)}) copy-start(f32[512]{0:T(512)} %param.11) | copy-start | bytes 6148
  25.6 7.7 %copy-start.6 = (f32[512]{0:T(512)S(1)}, f32[512]{0:T(512)}, u32[]{:S(2)}) copy-start(f32[512]{0:T(512)} %param.12) | copy-start | bytes 6148
  25.6 7.8 %copy-start.3 = (f32[512]{0:T(512)S(1)}, f32[512]{0:T(512)}, u32[]{:S(2)}) copy-start(f32[512]{0:T(512)} %param.9) | copy-start | bytes 6148
  25.6 7.8 %copy-start.4 = (f32[512]{0:T(512)S(1)}, f32[512]{0:T(512)}, u32[]{:S(2)}) copy-start(f32[512]{0:T(512)} %param.10) | copy-start | bytes 6148
  25.6 7.8 %copy-start.2 = (s32[2048,4]{0,1:T(4,128)S(1)}, s32[2048,4]{0,1:T(4,128)}, u32[]{:S(2)}) copy-start(s32[2048,4]{0,1:T(4,128)} %param.13) | copy-start | bytes 98308
  25.6 304.4 %all-to-all-start = ((bf16[256,3,8192]{0,1,2:T(4,128)(2,1)}), bf16[256,3,8192]{0,1,2:T(4,128)(2,1)}, u32[]{:S(2)}, u32[]{:S(2)}) async-start(bf16[256,3,8192]{0,1,2:T(4,128)(2,1)} %copy.16), calls=%async_computation | async-start | bytes 33554432 | tf_op jit(solution)/shard_map/all_to_all | solution.py:47
  603.6 2.0 copy-start
  603.6 3.2 copy-start.1
where the time goes:
time: 747 us; the launch traced here: 745 us
  waiting for transfers between devices  296 us (40%)
  local copies, waits for them, and re-layouts  212 us (28%)
  other arithmetic  130 us (17%)
  blocking collectives  98.9 us (13%)
  starting transfers between devices  7.58 us (1%)
    all_to_all x1, waiting for transfers between devices, local(): lax.all_to_all(fields, 'cell', split_axis=2, concat_axis=0, tiled=True)  296 us
    gather x4, local copies, waits for them, and re-layouts, pick(): return jnp.take(grads, rows[:, column], axis=0).astype(jnp.float32)  107 us
    reduce_sum x1, other arithmetic, sensitivity(): inner = jnp.sum(source * receiver, axis=1)  104 us
    psum x1, blocking collectives, local(): total_sq = lax.psum(partial_sq, 'cell')  98.9 us
    unnamed x16, local copies, waits for them, and re-layouts  55.5 us
    all_to_all x3, local copies, waits for them, and re-layouts, local(): lax.all_to_all(fields, 'cell', split_axis=2, concat_axis=0, tiled=True)  48.6 us
  transfers between devices with their start and end apart: 1, of which 1 were waited for; matrix products, arithmetic and copies ran while one was open for 0% of the time, Pallas kernels for 0%

commit v1 on v0

--- a/solution.py
+++ b/solution.py
@@ -2,6 +2,28 @@
 import jax.numpy as jnp
 from jax import lax
 from jax.sharding import PartitionSpec as P
+
+
+def in_blocks(shard, dim, size):
+    before, after = (shard.shape[:dim], shard.shape[dim + 1 :])
+    return jnp.moveaxis(shard.reshape(*before, size, -1, *after), dim, 0)
+
+
+def joined_along(pieces, dim):
+    pieces = jnp.moveaxis(pieces, 0, dim)
+    dims = pieces.shape
+    return pieces.reshape(*dims[:dim], dims[dim] * dims[dim + 1], *dims[dim + 2 :])
+
+
+def exchange_in_pairs(x, axis, split_dim, concat_dim):
+    count, position = (lax.axis_size(axis), lax.axis_index(axis))
+    pieces = in_blocks(x, split_dim, count)
+    finished = [pieces[position]]
+    for turn in range(1, count):
+        sent = pieces[position ^ turn]
+        finished.append(lax.ppermute(sent, axis, [(i, i ^ turn) for i in range(count)]))
+    pieces = jnp.stack(finished)[position ^ jnp.arange(count)]
+    return joined_along(pieces, concat_dim)
 
 
 def sensitivity(grads, horiz, vertical, tilt_angle, azimuth, rows):
@@ -44,7 +66,7 @@
 def local(fields, horiz, vertical, tilt_angle, azimuth, electrode_quads):
     shards = lax.axis_size("cell")
     cell_dev = horiz.shape[0]
-    local_fields = lax.all_to_all(fields, "cell", split_axis=2, concat_axis=0, tiled=True)
+    local_fields = exchange_in_pairs(fields, "cell", 2, 0)
     values = sensitivity(local_fields, horiz, vertical, tilt_angle, azimuth, electrode_quads)
     partial_sq = jnp.sum(values * values, axis=(1, 2))
     total_sq = lax.psum(partial_sq, "cell")

time: 747 us -> 712 us (0.953)
  waiting for transfers between devices: 296 us -> 184 us
  local copies, waits for them, and re-layouts: 212 us -> 285 us
  starting transfers between devices: 7.58 us -> 23 us
  blocking collectives: 98.9 us -> 86.6 us
    all_to_all x1 -> x0, waiting for transfers between devices: 296 us -> none  [local(): lax.all_to_all(fields, 'cell', split_axis=2, concat_axis=0, tiled=True)]
    ppermute x0 -> x15, waiting for transfers between devices: none -> 184 us  [exchange_in_pairs(): lax.ppermute(sent, axis, [(i, i ^ turn) for i in range(count)])]
    reshape x0 -> x1, local copies, waits for them, and re-layouts: none -> 54.1 us  [joined_along(): pieces.reshape(*dims[:dim], dims[dim] * dims[dim + 1], *dims[dim + 2:])]
    all_to_all x3 -> x0, local copies, waits for them, and re-layouts: 48.6 us -> none  [local(): lax.all_to_all(fields, 'cell', split_axis=2, concat_axis=0, tiled=True)]
    another operation x0 -> x18, local copies, waits for them, and re-layouts: none -> 38.7 us
    ppermute x0 -> x15, starting transfers between devices: none -> 23 us  [exchange_in_pairs(): lax.ppermute(sent, axis, [(i, i ^ turn) for i in range(count)])]
    gather x0 -> x2, local copies, waits for them, and re-layouts: none -> 17.3 us  [exchange_in_pairs(): pieces = jnp.stack(finished)[position ^ jnp.arange(count)]]
    unnamed x16 -> x31, local copies, waits for them, and re-layouts: 55.5 us -> 68.2 us
  transfers between devices with their start and end apart: 1 -> 15, of which waited for: 1 -> 5; matrix products, arithmetic and copies ran while one was open for 0% -> 7% of each run, Pallas kernels for 0% -> 0%
where the time goes in v1:
time: 712 us; the launch traced here: 710 us
  local copies, waits for them, and re-layouts  285 us (40%)
  waiting for transfers between devices  184 us (26%)
  other arithmetic  130 us (18%)
  blocking collectives  86.6 us (12%)
  starting transfers between devices  23 us (3%)
    ppermute x15, waiting for transfers between devices, exchange_in_pairs(): lax.ppermute(sent, axis, [(i, i ^ turn) for i in range(count)])  184 us
    gather x4, local copies, waits for them, and re-layouts, pick(): return jnp.take(grads, rows[:, column], axis=0).astype(jnp.float32)  107 us
    reduce_sum x1, other arithmetic, sensitivity(): inner = jnp.sum(source * receiver, axis=1)  104 us
    psum x1, blocking collectives, local(): total_sq = lax.psum(partial_sq, 'cell')  86.6 us
    unnamed x31, local copies, waits for them, and re-layouts  68.2 us
    reshape x1, local copies, waits for them, and re-layouts, joined_along(): pieces.reshape(*dims[:dim], dims[dim] * dims[dim + 1], *dims[dim + 2:])  54.1 us
    another operation x17, local copies, waits for them, and re-layouts  37.7 us
    ppermute x15, starting transfers between devices, exchange_in_pairs(): lax.ppermute(sent, axis, [(i, i ^ turn) for i in range(count)])  23 us
  transfers between devices with their start and end apart: 15, of which 5 were waited for; matrix products, arithmetic and copies ran while one was open for 7% of the time, Pallas kernels for 0%

profile of v1, /device:TPU:0, one launch (start us, length us, event | category | flops | bytes accessed | tf_op | source)
XLA Modules:
  0.0 710.4 jit_solution(14091153309603280939)
XLA Ops:
  0.7 16.6 %copy.10 = bf16[256,3,8192]{0,2,1:T(8,128)(2,1)} copy(bf16[256,3,8192]{2,0,1:T(8,128)(2,1)} %param.8) | data formatting | bytes 25165824 | tf_op args[0]
  17.4 8.0 %constant_dynamic-slice_fusion = (bf16[256,3,1,512]{0,3,2,1:T(8,128)(2,1)S(1)}, bf16[256,3,1,512]{0,3,2,1:T(8,128)(2,1)S(1)}, bf16[256,3,1,512]{0,3,2,1:T(8,128)...) fusion(bf16[256,3,16,512]{0,3,2,1:T(8,128)(2,1)} %bitcast.102, ...), kind=kLoop, calls=%fused_computation.68 | loop fusion | bytes 25165888 | tf_op jit(solution)/shard_map/dynamic-slice.15
  28.1 2.3 copy.13
  30.4 2.5 collective-permute-start.1
  35.4 2.3 copy.15
  42.2 2.3 copy.11
  49.1 2.3 copy.19
  51.4 2.3 copy.20
  56.0 2.3 copy.22
  62.5 2.6 collective-permute-start.5
  69.4 2.7 collective-permute-start.7
  76.2 31.6 %collective-permute-done.4 = bf16[256,3,512]{2,0,1:T(8,128)(2,1)} collective-permute-done((bf16[256,3,512]{2,0,1:T(8,128)(2,1)}, bf16[256,3,512]{2,0,1:T(8,128)(2,1)}, u32[]{:S(2)}, u32[]{:S(2)}) %collective-permute-start.4) | collective-permute-done | bytes 786464 | tf_op jit(solution)/shard_map/ppermute | solution.py:24
  107.8 4.0 collective-permute-start.9
  113.9 13.1 %collective-permute-done.5 = bf16[256,3,512]{2,0,1:T(8,128)(2,1)S(1)} collective-permute-done((bf16[256,3,512]{2,0,1:T(8,128)(2,1)}, bf16[256,3,512]{2,0,1:T(8,128)(2,1)S(1)}, u32[]{:S(2)}, u32[]{:S(2)}) %collective-permute-start.5) | collective-permute-done | bytes 786464 | tf_op jit(solution)/shard_map/ppermute | solution.py:24
  128.1 14.4 %collective-permute-done.6 = bf16[256,3,512]{2,0,1:T(8,128)(2,1)S(1)} collective-permute-done((bf16[256,3,512]{2,0,1:T(8,128)(2,1)}, bf16[256,3,512]{2,0,1:T(8,128)(2,1)S(1)}, u32[]{:S(2)}, u32[]{:S(2)}) %collective-permute-start.6) | collective-permute-done | bytes 786464 | tf_op jit(solution)/shard_map/ppermute | solution.py:24
  142.5 3.6 collective-permute-start.11
  148.4 3.5 collective-permute-start.13
  152.8 93.5 %collective-permute-done.9 = bf16[256,3,512]{2,0,1:T(8,128)(2,1)S(1)} collective-permute-done((bf16[256,3,512]{2,0,1:T(8,128)(2,1)}, bf16[256,3,512]{2,0,1:T(8,128)(2,1)S(1)}, u32[]{:S(2)}, u32[]{:S(2)}) %collective-permute-start.9) | collective-permute-done | bytes 786464 | tf_op jit(solution)/shard_map/ppermute | solution.py:24
  248.2 31.7 %collective-permute-done.10 = bf16[256,3,512]{2,0,1:T(8,128)(2,1)S(1)} collective-permute-done((bf16[256,3,512]{2,0,1:T(8,128)(2,1)}, bf16[256,3,512]{2,0,1:T(8,128)(2,1)S(1)}, u32[]{:S(2)}, u32[]{:S(2)}) %collective-permute-start.10) | collective-permute-done | bytes 786464 | tf_op jit(solution)/shard_map/ppermute | solution.py:24
  284.7 11.0 %gather_fusion = bf16[16,256,3,512]{3,1,2,0:T(8,128)(2,1)} fusion(bf16[16,256,3,512]{3,1,2,0:T(8,128)(2,1)} %bitcast_dynamic-update-slice_fusion, s32[1024]{0:T(1024)S(1)} %pad_clamp_fusion), kind=kCustom, calls=%fused_computation.4 | custom fusion | bytes 25165888 | tf_op jit(solution)/shard_map/gather | solution.py:25
  295.7 6.3 copy.27
  302.0 54.1 %copy.28 = bf16[4096,3,512]{2,1,0:T(4,128)(2,1)} copy(bf16[4096,3,512]{2,0,1:T(8,128)(2,1)S(1)} %bitcast.101) | data formatting | bytes 25165824 | tf_op jit(solution)/shard_map/reshape | solution.py:15
  356.1 26.8 %gather_fusion.2 = bf16[2048,3,512]{2,1,0:T(4,128)(2,1)} fusion(bf16[4096,3,512]{2,1,0:T(4,128)(2,1)} %copy.28, s32[2048]{0:T(1024)S(1)} %get-tuple-element.58), kind=kCustom, calls=%fused_computation.1.clone | custom fusion | bytes 12591104 | tf_op jit(solution)/shard_map/jit(_take)/gather | solution.py:32
  382.9 26.8 %gather_fusion.3 = bf16[2048,3,512]{2,1,0:T(4,128)(2,1)} fusion(bf16[4096,3,512]{2,1,0:T(4,128)(2,1)} %copy.28, s32[2048]{0:T(1024)S(1)} %get-tuple-element.59), kind=kCustom, calls=%fused_computation.2.clone | custom fusion | bytes 12591104 | tf_op jit(solution)/shard_map/jit(_take)/gather | solution.py:32
  409.7 26.8 %gather_fusion.4 = bf16[2048,3,512]{2,1,0:T(4,128)(2,1)} fusion(bf16[4096,3,512]{2,1,0:T(4,128)(2,1)} %copy.28, s32[2048]{0:T(1024)S(1)} %get-tuple-element.60), kind=kCustom, calls=%fused_computation.3.clone | custom fusion | bytes 12591104 | tf_op jit(solution)/shard_map/jit(_take)/gather | solution.py:32
  436.5 26.7 %gather_fusion.1 = bf16[2048,3,512]{2,1,0:T(4,128)(2,1)} fusion(bf16[4096,3,512]{2,1,0:T(4,128)(2,1)} %copy.28, s32[2048]{0:T(1024)S(1)} %get-tuple-element.57), kind=kCustom, calls=%fused_computation.clone | custom fusion | bytes 12591104 | tf_op jit(solution)/shard_map/jit(_take)/gather | solution.py:32
  463.2 103.7 %multiply_reduce_fusion.8 = (f32[2048,512]{1,0:T(8,128)}, f32[2048,512]{1,0:T(8,128)}, f32[2048,512]{1,0:T(8,128)}, f32[2048,512]{1,0:T(8,128)}, f32[2048,512]{1...) fusion(bf16[2048,3,512]{2,1,0:T(4,128)(2,1)} %gather_fusion.1, pred[2048]{0:T(1024)(128)(4,1)S(1)} %get-tuple-element.66, ...), kind=kLoop, calls=%fused_computation.14 | loop fusion | flops 68157440 | bytes 54552576 | tf_op jit(solution)/shard_map/reduce_sum | solution.py:53
  566.9 14.1 %fusion.5 = (f32[2048,1,512]{2,0,1:T(8,128)S(1)}, f32[2048,1,512]{2,0,1:T(8,128)S(1)}, f32[2048,1,512]{2,0,1:T(8,128)}, f32[2048,1,512]{2,0,1:T(8,128)}) fusion(f32[2048,512]{1,0:T(8,128)} %get-tuple-element.12, f32[2048,512]{1,0:T(8,128)} %get-tuple-element.13, f32[2048,512]{1,0:T(8,128)} %get-tuple-element.7, f32[512]{0:T(512)S(1)} %get-tuple-element.48, ...), kind=kLoop, calls=%fused_computation.33 | loop fusion | flops 13631488 | bytes 46143488 | tf_op jit(solution)/shard_map/mul | solution.py:57
  584.2 4.6 multiply_reduce_fusion.1
  588.8 86.6 %psum.7 = f32[2048]{0:T(1024)S(1)} all-reduce(f32[2048]{0:T(1024)S(1)} %multiply_reduce_fusion.1), channel_id=1, replica_groups=mesh['grp'=2,'cell'=16] {'cell'}, use_global_device_ids=true, to_apply=%region_8.10 | all-reduce | flops 2048 | bytes 16384 | tf_op jit(solution)/shard_map/psum | solution.py:72
  675.4 7.7 %multiply_reduce_fusion = (f32[512]{0:T(512)}, bf16[2048,4,512]{2,0,1:T(8,128)(2,1)S(1)}) fusion(f32[2048]{0:T(1024)S(1)} %add_rsqrt_fusion, f32[2048,1,512]{2,0,1:T(8,128)} %get-tuple-element.36, f32[2048,1,512]{2,0,1:T(8,128)} %get-tuple-element.37, f32[2048,1,512]{2,0,1:T(8,128)} %copy-done.1, f32[2048,1,512]{2,0,1:T(8,128)} %copy-done), kind=kLoop, calls=%fused_computation.6 | loop fusion | flops 29359616 | bytes 25176064 | tf_op jit(solution)/shard_map/reduce_sum | solution.py:75
  683.1 27.3 %copy.32 = bf16[2048,4,512]{2,1,0:T(4,128)(2,1)} copy(bf16[2048,4,512]{2,0,1:T(8,128)(2,1)S(1)} %get-tuple-element.15) | data formatting | bytes 16777216
  (73 shorter events, 45.3 us)
Async XLA Ops:
  17.3 24.5 %copy-start.2 = (s32[2048,4]{0,1:T(4,128)S(1)}, s32[2048,4]{0,1:T(4,128)}, u32[]{:S(2)}) copy-start(s32[2048,4]{0,1:T(4,128)} %param.13) | copy-start | bytes 98308
  17.3 24.6 %copy-start.5 = (f32[512]{0:T(512)S(1)}, f32[512]{0:T(512)}, u32[]{:S(2)}) copy-start(f32[512]{0:T(512)} %param.11) | copy-start | bytes 6148
  17.3 24.6 %copy-start.6 = (f32[512]{0:T(512)S(1)}, f32[512]{0:T(512)}, u32[]{:S(2)}) copy-start(f32[512]{0:T(512)} %param.12) | copy-start | bytes 6148
  17.3 24.8 %copy-start.3 = (f32[512]{0:T(512)S(1)}, f32[512]{0:T(512)}, u32[]{:S(2)}) copy-start(f32[512]{0:T(512)} %param.9) | copy-start | bytes 6148
  17.3 24.8 %copy-start.4 = (f32[512]{0:T(512)S(1)}, f32[512]{0:T(512)}, u32[]{:S(2)}) copy-start(f32[512]{0:T(512)} %param.10) | copy-start | bytes 6148
  27.7 34.8 %collective-permute-start = (bf16[256,3,512]{2,0,1:T(8,128)(2,1)}, bf16[256,3,512]{2,0,1:T(8,128)(2,1)}, u32[]{:S(2)}, u32[]{:S(2)}) collective-permute-start(bf16[256,3,512]{2,0,1:T(8,128)(2,1)} %bitcast.113), channel_id=1, source_target_pairs={{0,1},{1,0},{2,3},{3,2},{4,5},{5,4},{6,7},{7,6},{8,9},{9,8},{10,11... | collective-permute-start | bytes 2359304 | tf_op jit(solution)/shard_map/ppermute | solution.py:24
  30.4 36.7 %collective-permute-start.1 = (bf16[256,3,512]{2,0,1:T(8,128)(2,1)}, bf16[256,3,512]{2,0,1:T(8,128)(2,1)}, u32[]{:S(2)}, u32[]{:S(2)}) collective-permute-start(bf16[256,3,512]{2,0,1:T(8,128)(2,1)} %bitcast.111), channel_id=1, source_target_pairs={{0,2},{1,3},{2,0},{3,1},{4,6},{5,7},{6,4},{7,5},{8,10},{9,11},{10,... | collective-permute-start | bytes 2359304 | tf_op jit(solution)/shard_map/ppermute | solution.py:24
  35.3 34.1 %collective-permute-start.2 = (bf16[256,3,512]{2,0,1:T(8,128)(2,1)}, bf16[256,3,512]{2,0,1:T(8,128)(2,1)}, u32[]{:S(2)}, u32[]{:S(2)}) collective-permute-start(bf16[256,3,512]{2,0,1:T(8,128)(2,1)} %bitcast.110), channel_id=1, source_target_pairs={{0,3},{1,2},{2,1},{3,0},{4,7},{5,6},{6,5},{7,4},{8,11},{9,10},{10,... | collective-permute-start | bytes 2359304 | tf_op jit(solution)/shard_map/ppermute | solution.py:24
  37.7 36.4 %collective-permute-start.3 = (bf16[256,3,512]{2,0,1:T(8,128)(2,1)}, bf16[256,3,512]{2,0,1:T(8,128)(2,1)}, u32[]{:S(2)}, u32[]{:S(2)}) collective-permute-start(bf16[256,3,512]{2,0,1:T(8,128)(2,1)} %bitcast.108), channel_id=1, source_target_pairs={{0,4},{1,5},{2,6},{3,7},{4,0},{5,1},{6,2},{7,3},{8,12},{9,13},{10,... | collective-permute-start | bytes 2359304 | tf_op jit(solution)/shard_map/ppermute | solution.py:24
  41.8 66.0 %collective-permute-start.4 = (bf16[256,3,512]{2,0,1:T(8,128)(2,1)}, bf16[256,3,512]{2,0,1:T(8,128)(2,1)}, u32[]{:S(2)}, u32[]{:S(2)}) collective-permute-start(bf16[256,3,512]{2,0,1:T(8,128)(2,1)} %bitcast.106), channel_id=1, source_target_pairs={{0,5},{1,4},{2,7},{3,6},{4,1},{5,0},{6,3},{7,2},{8,13},{9,12},{10,... | collective-permute-start | bytes 2359304 | tf_op jit(solution)/shard_map/ppermute | solution.py:24
  62.5 64.5 %collective-permute-start.5 = (bf16[256,3,512]{2,0,1:T(8,128)(2,1)}, bf16[256,3,512]{2,0,1:T(8,128)(2,1)S(1)}, u32[]{:S(2)}, u32[]{:S(2)}) collective-permute-start(bf16[256,3,512]{2,0,1:T(8,128)(2,1)} %bitcast.117), channel_id=1, source_target_pairs={{0,6},{1,7},{2,4},{3,5},{4,2},{5,3},{6,0},{7,1},{8,14},{9,15},{10,... | collective-permute-start | bytes 2359304 | tf_op jit(solution)/shard_map/ppermute | solution.py:24
  67.2 75.4 %collective-permute-start.6 = (bf16[256,3,512]{2,0,1:T(8,128)(2,1)}, bf16[256,3,512]{2,0,1:T(8,128)(2,1)S(1)}, u32[]{:S(2)}, u32[]{:S(2)}) collective-permute-start(bf16[256,3,512]{2,0,1:T(8,128)(2,1)} %bitcast.116), channel_id=1, source_target_pairs={{0,7},{1,6},{2,5},{3,4},{4,3},{5,2},{6,1},{7,0},{8,15},{9,14},{10,... | collective-permute-start | bytes 2359304 | tf_op jit(solution)/shard_map/ppermute | solution.py:24
  69.4 77.7 %collective-permute-start.7 = (bf16[256,3,512]{2,0,1:T(8,128)(2,1)}, bf16[256,3,512]{2,0,1:T(8,128)(2,1)S(1)}, u32[]{:S(2)}, u32[]{:S(2)}) collective-permute-start(bf16[256,3,512]{2,0,1:T(8,128)(2,1)} %bitcast.115), channel_id=1, source_target_pairs={{0,8},{1,9},{2,10},{3,11},{4,12},{5,13},{6,14},{7,15},{8,0},{9,1},... | collective-permute-start | bytes 2359304 | tf_op jit(solution)/shard_map/ppermute | solution.py:24
  74.1 74.2 %collective-permute-start.8 = (bf16[256,3,512]{2,0,1:T(8,128)(2,1)}, bf16[256,3,512]{2,0,1:T(8,128)(2,1)S(1)}, u32[]{:S(2)}, u32[]{:S(2)}) collective-permute-start(bf16[256,3,512]{2,0,1:T(8,128)(2,1)} %bitcast.114), channel_id=1, source_target_pairs={{0,9},{1,8},{2,11},{3,10},{4,13},{5,12},{6,15},{7,14},{8,1},{9,0},... | collective-permute-start | bytes 2359304 | tf_op jit(solution)/shard_map/ppermute | solution.py:24
  107.8 138.5 %collective-permute-start.9 = (bf16[256,3,512]{2,0,1:T(8,128)(2,1)}, bf16[256,3,512]{2,0,1:T(8,128)(2,1)S(1)}, u32[]{:S(2)}, u32[]{:S(2)}) collective-permute-start(bf16[256,3,512]{2,0,1:T(8,128)(2,1)} %bitcast.112), channel_id=1, source_target_pairs={{0,10},{1,11},{2,8},{3,9},{4,14},{5,15},{6,12},{7,13},{8,2},{9,3},... | collective-permute-start | bytes 2359304 | tf_op jit(solution)/shard_map/ppermute | solution.py:24
  127.0 152.9 %collective-permute-start.10 = (bf16[256,3,512]{2,0,1:T(8,128)(2,1)}, bf16[256,3,512]{2,0,1:T(8,128)(2,1)S(1)}, u32[]{:S(2)}, u32[]{:S(2)}) collective-permute-start(bf16[256,3,512]{2,0,1:T(8,128)(2,1)} %bitcast.109), channel_id=1, source_target_pairs={{0,11},{1,10},{2,9},{3,8},{4,15},{5,14},{6,13},{7,12},{8,3},{9,2},... | collective-permute-start | bytes 2359304 | tf_op jit(solution)/shard_map/ppermute | solution.py:24
  142.5 138.4 %collective-permute-start.11 = (bf16[256,3,512]{2,0,1:T(8,128)(2,1)}, bf16[256,3,512]{2,0,1:T(8,128)(2,1)S(1)}, u32[]{:S(2)}, u32[]{:S(2)}) collective-permute-start(bf16[256,3,512]{2,0,1:T(8,128)(2,1)} %bitcast.107), channel_id=1, source_target_pairs={{0,12},{1,13},{2,14},{3,15},{4,8},{5,9},{6,10},{7,11},{8,4},{9,5},... | collective-permute-start | bytes 2359304 | tf_op jit(solution)/shard_map/ppermute | solution.py:24
  147.1 134.8 %collective-permute-start.12 = (bf16[256,3,512]{2,0,1:T(8,128)(2,1)S(1)}, bf16[256,3,512]{2,0,1:T(8,128)(2,1)S(1)}, u32[]{:S(2)}, u32[]{:S(2)}) collective-permute-start(bf16[256,3,512]{2,0,1:T(8,128)(2,1)S(1)} %bitcast.105), channel_id=1, source_target_pairs={{0,13},{1,12},{2,15},{3,14},{4,9},{5,8},{6,11},{7,10},{8,5},{9,4},... | collective-permute-start | bytes 2359304 | tf_op jit(solution)/shard_map/ppermute | solution.py:24
  148.4 134.4 %collective-permute-start.13 = (bf16[256,3,512]{2,0,1:T(8,128)(2,1)S(1)}, bf16[256,3,512]{2,0,1:T(8,128)(2,1)S(1)}, u32[]{:S(2)}, u32[]{:S(2)}) collective-permute-start(bf16[256,3,512]{2,0,1:T(8,128)(2,1)S(1)} %bitcast.104), channel_id=1, source_target_pairs={{0,14},{1,15},{2,12},{3,13},{4,10},{5,11},{6,8},{7,9},{8,6},{9,7},... | collective-permute-start | bytes 2359304 | tf_op jit(solution)/shard_map/ppermute | solution.py:24
  246.2 37.5 %collective-permute-start.14 = (bf16[256,3,512]{2,0,1:T(8,128)(2,1)S(1)}, bf16[256,3,512]{2,0,1:T(8,128)(2,1)S(1)}, u32[]{:S(2)}, u32[]{:S(2)}) collective-permute-start(bf16[256,3,512]{2,0,1:T(8,128)(2,1)S(1)} %bitcast.103), channel_id=1, source_target_pairs={{0,15},{1,14},{2,13},{3,12},{4,11},{5,10},{6,9},{7,8},{8,7},{9,6},... | collective-permute-start | bytes 2359304 | tf_op jit(solution)/shard_map/ppermute | solution.py:24
  581.0 2.0 copy-start
  581.0 3.2 copy-start.1
